TPU v7x, 32 devices: a whole 2x2x4 slice. The times are simulated.
32 devices in a mesh: groups: 2 (over y), zone: 4 (over z), scen: 2 (over x), hour: 2 (over core).
Axes of the slice: x: 2, y: 2, z: 4, core: 2. Of those that a mesh axis runs over, the one named last changes fastest.
Arguments:
- forcing: bfloat16 [1024, 48, 64], P(('groups', 'zone', 'scen', 'hour')), parts along dimension 0, may hold values from -3 to 3
- response: bfloat16 [48, 64, 8192], P('hour', None, ('groups', 'zone')), parts along dimension 2, may hold values from -0.75 to 0.75
- window_params: float32 [128, 64], P('groups'), parts along dimension 0, may hold values from 0.5 to 1.5
- building_map: int32 [8192], P(('groups', 'zone')), parts along dimension 0, may hold values from 0 to 1023
- owner_ids: int32 [2048], P('groups'), parts along dimension 0, may hold values from 0 to 63
- band_ids: int32 [48, 8192], P('hour', ('groups', 'zone')), parts along dimension 1, may hold values from 0 to 7
- floor_area: float32 [8192], P(('groups', 'zone')), parts along dimension 0, may hold values from 0.5 to 18, as said below
Outputs:
- sensitivity: float32 [128, 64], P(('groups', 'zone', 'scen', 'hour')), parts along dimension 0
- objective: float32 [2], P('groups'), parts along dimension 0
There are 2 independent parts, one for each index of `groups`. A program takes and returns all parts, laid end to end along the dimension named above; each array names one. Nothing has to cross between parts.
Inputs may be any that keep to these rules, and one draw needn't show every extreme that they name: `floor_area`: floor areas are positive.
All inputs are finite; a program needn't handle non-finite values.
Results may differ from a plain program's by a relative error of at most 0.0006.
Values may be sent and summed in bfloat16 or wider, within the bound.
A program may use at most 128 MiB of HBM per device.

v0:
```python
import math

import jax
import jax.numpy as jnp
from jax import lax
from jax.sharding import PartitionSpec as P

SHARPNESS = 200.0


def joined(value, axis, join):
    pieces = jax.tree.map(lambda part: lax.all_gather(part, axis), value)
    head = jax.tree.map(lambda part: part[0], pieces)
    tail = jax.tree.map(lambda part: part[1:], pieces)
    running, _ = lax.scan(lambda running, share: (join(running, share), None), head, tail)
    return running


def merge_softmax(first, second):
    highest = jnp.maximum(first[0], second[0])
    return (
        highest,
        first[1] * jnp.exp(first[0] - highest) + second[1] * jnp.exp(second[0] - highest),
    )


def on_device(forcing, response, window_params, building_map, owner_ids, band_ids, floor_area):
    hour_local = response.shape[0]
    width = response.shape[1]
    zone_local = response.shape[2]
    hours_total = hour_local * lax.axis_size("hour")
    hour_first = lax.axis_index("hour") * hour_local
    positions = (hour_first + jnp.arange(hour_local)).astype(jnp.float32)
    occupant_level = 1.0 + 2.0 * positions / (hours_total - 1)
    candidate_plan = jnp.take(owner_ids, building_map)
    zone_parameters = jnp.take(window_params, candidate_plan, axis=0)
    coeff = (response.astype(jnp.float32) * zone_parameters.T[None, :, :]).astype(jnp.bfloat16)
    band_low = 0.25 * (band_ids.astype(jnp.float32) - 3.5) - 0.5
    band_high = band_low + 1.0
    zone_weight = occupant_level[:, None] * floor_area[None, :]
    block_count = hour_local // 8
    mine = lax.all_to_all(forcing, "hour", split_axis=1, concat_axis=0, tiled=True)

    def inside_climate_state(outlook_records, initial_clock_time):
        record_elements = lax.slice_in_dim(
            outlook_records, initial_clock_time, initial_clock_time + 8, axis=1
        )
        thermal_demand = jnp.einsum(
            "shp,hpz->hsz",
            record_elements,
            coeff[initial_clock_time : initial_clock_time + 8],
            preferred_element_type=jnp.float32,
        )
        return (thermal_demand, record_elements)

    weight_part = (jnp.sum(floor_area) * jnp.sum(occupant_level)).reshape(1)
    outlook_records = lax.all_gather(mine, "zone", axis=0, tiled=True)
    sums = jnp.zeros((outlook_records.shape[0],), jnp.float32)
    for hour_block in range(block_count):
        initial_clock_time = hour_block * 8
        thermal_demand, record_elements = inside_climate_state(outlook_records, initial_clock_time)
        low = band_low[initial_clock_time : initial_clock_time + 8][:, None, :]
        high = band_high[initial_clock_time : initial_clock_time + 8][:, None, :]
        penalty = jax.nn.softplus(thermal_demand - high) + jax.nn.softplus(low - thermal_demand)
        sums = sums + jnp.sum(
            penalty * zone_weight[initial_clock_time : initial_clock_time + 8][:, None, :],
            axis=(0, 2),
        )
    loss_sum, weight_total = lax.psum((sums, weight_part), ("zone", "hour"))
    scores = SHARPNESS * loss_sum / weight_total[0]
    local_peak = jnp.max(scores)
    peak_score, exp_total = joined(
        (local_peak, jnp.sum(jnp.exp(scores - local_peak))), "scen", merge_softmax
    )
    objective = ((peak_score + jnp.log(exp_total)) / SHARPNESS).reshape(1)
    scen_weight = jnp.exp(scores - peak_score) / exp_total / weight_total[0]
    empty = jnp.zeros((width, zone_local), jnp.float32)
    accumulated = empty
    outlook_records = lax.all_gather(mine, "zone", axis=0, tiled=True)
    for hour_block in range(block_count):
        initial_clock_time = hour_block * 8
        thermal_demand, record_elements = inside_climate_state(outlook_records, initial_clock_time)
        low = band_low[initial_clock_time : initial_clock_time + 8][:, None, :]
        high = band_high[initial_clock_time : initial_clock_time + 8][:, None, :]
        slope = jax.nn.sigmoid(thermal_demand - high) - jax.nn.sigmoid(low - thermal_demand)
        adjoint = (
            slope
            * scen_weight[None, :, None]
            * zone_weight[initial_clock_time : initial_clock_time + 8][:, None, :]
        ).astype(jnp.bfloat16)
        mixed = jnp.einsum(
            "shp,hsz->hpz", record_elements, adjoint, preferred_element_type=jnp.float32
        )
        accumulated = accumulated + jnp.sum(
            response[initial_clock_time : initial_clock_time + 8].astype(jnp.float32) * mixed,
            axis=0,
        )
    zones_all = zone_local * lax.axis_size("zone")
    designs = window_params.shape[0]
    gain = math.sqrt(width * zones_all * hours_total * designs)
    zone_rows = accumulated.T
    owners_local = designs // (
        lax.axis_size("zone") * lax.axis_size("scen") * lax.axis_size("hour")
    )
    onehot = (
        candidate_plan[:, None]
        == jnp.arange(owners_local * lax.axis_size(("zone", "scen", "hour")))[None, :]
    ).astype(jnp.float32)
    sensitivity = lax.psum_scatter(
        gain * jnp.dot(onehot.T, zone_rows, precision=lax.Precision.HIGHEST),
        ("zone", "scen", "hour"),
        scatter_dimension=0,
        tiled=True,
    )
    return (sensitivity, objective)


def solution(mesh):
    in_specs = (
        P(("groups", "zone", "scen", "hour"), None, None),
        P("hour", None, ("groups", "zone")),
        P("groups", None),
        P(("groups", "zone")),
        P("groups"),
        P("hour", ("groups", "zone")),
        P(("groups", "zone")),
    )
    out_specs = (P(("groups", "zone", "scen", "hour"), None), P("groups"))
    return jax.shard_map(
        on_device, mesh=mesh, in_specs=in_specs, out_specs=out_specs, check_vma=False
    )
```

profile of v0, /device:TPU:0, one launch (start us, length us, event | category | flops | bytes accessed | tf_op | source)
XLA Modules:
  0.0 207.4 jit_solution(13071616913442641954)
XLA Ops:
  0.7 1.2 copy.37
  1.8 1.0 reshape.77
  2.9 3.4 %all-to-all-start = ((bf16[2,2,24576]{2,1,0:T(2,128)(2,1)}), bf16[2,2,24576]{2,1,0:T(2,128)(2,1)S(1)}, u32[]{:S(2)}, u32[]{:S(2)}) async-start(bf16[2,2,24576]{2,1,0:T(2,128)(2,1)} %reshape.77), calls=%async_computation | async-start | bytes 393216 | tf_op jit(solution)/shard_map/all_to_all | solution.py:42
  6.3 1.5 all-to-all-done
  7.8 0.3 reshape.78
  8.2 31.7 %all_gather.16 = bf16[256,24,64]{2,1,0:T(8,128)(2,1)S(1)} all-gather(bf16[64,24,64]{2,1,0:T(8,128)(2,1)S(1)} %bitcast.231), channel_id=1, replica_groups=mesh['groups'=2,'zone'=4,'scen'=2,'hour'=2] {'zone'}, dimensions={0}, use_global_device_ids=true | all-gather | bytes 983040 | tf_op jit(solution)/shard_map/all_gather | solution.py:79
  40.2 0.3 copy.35
  40.6 0.6 multiply_add_fusion
  41.3 4.5 %gather_fusion = s32[1024]{0:T(1024)S(1)} fusion(s32[1024]{0:T(1024)S(1)} %copy-done.1, s32[1024]{0:T(1024)S(1)} %fusion.88), kind=kCustom, calls=%fused_computation | custom fusion | bytes 12288 | tf_op jit(solution)/shard_map/jit(_take)/gather | solution.py:35
  45.9 2.8 %gather_fusion.1 = f32[1024,64]{1,0:T(8,128)S(1)} fusion(f32[64,64]{1,0:T(8,128)S(1)} %copy-done, s32[1024]{0:T(1024)S(1)} %fusion.89), kind=kCustom, calls=%fused_computation.1 | custom fusion | bytes 528384 | tf_op jit(solution)/shard_map/jit(_take)/gather | solution.py:36
  49.1 0.3 copy.33
  49.5 0.3 copy.34
  49.8 0.6 reduce_sum.84
  51.7 13.8 %fusion.8 = (f32[256]{0:T(256)S(1)}, f32[8,1024,256]{2,1,0:T(8,128)}) fusion(f32[8,1024]{1,0:T(8,128)S(1)} %get-tuple-element.35, f32[8,1024]{1,0:T(8,128)S(1)} %get-tuple-element.52, f32[8,1024]{1,0:T(8,128)S(1)} %get-tuple-element.29, bf16[256,8,64]{0,2,1:T(8,128)(2,1)S(1)} %copy.35, bf16[24,64,1024]{2,1,0:T(8,128)(2,1)} %param.8, f32[64,1024]{1,0:T(8,128)S(1)} %copy.19), kind=kOutput, calls=%fused_computation.16 | convolution fusion | flops 308805376 | bytes 12157952 | tf_op jit(solution)/shard_map/shp,hpz->hsz/dot_general | solution.py:48
  65.5 13.3 %fusion.2 = (f32[256]{0:T(256)S(1)}, f32[8,1024,256]{2,1,0:T(8,128)}) fusion(f32[8,1024]{1,0:T(8,128)S(1)} %get-tuple-element.36, f32[8,1024]{1,0:T(8,128)S(1)} %get-tuple-element.51, f32[8,1024]{1,0:T(8,128)S(1)} %get-tuple-element.30, bf16[256,8,64]{0,2,1:T(8,128)(2,1)S(1)} %copy.33, bf16[24,64,1024]{2,1,0:T(8,128)(2,1)S(1)} %copy-done.5, ...), kind=kOutput, calls=%fused_computation.10 | convolution fusion | flops 308805376 | bytes 12157952 | tf_op jit(solution)/shard_map/shp,hpz->hsz/dot_general | solution.py:48
  78.8 13.2 %fusion.5 = (f32[256]{0:T(256)S(1)}, f32[8,1024,256]{2,1,0:T(8,128)}) fusion(f32[8,1024]{1,0:T(8,128)S(1)} %get-tuple-element.34, f32[8,1024]{1,0:T(8,128)S(1)} %get-tuple-element.53, f32[8,1024]{1,0:T(8,128)S(1)} %get-tuple-element.28, bf16[256,8,64]{0,2,1:T(8,128)(2,1)S(1)} %copy.34, bf16[24,64,1024]{2,1,0:T(8,128)(2,1)S(1)} %copy-done.5, ...), kind=kOutput, calls=%fused_computation.13 | convolution fusion | flops 308805376 | bytes 12157952 | tf_op jit(solution)/shard_map/shp,hpz->hsz/dot_general | solution.py:48
  92.0 16.5 %all-reduce.3 = (f32[256]{0:T(256)S(1)}, f32[]{:T(128)}) all-reduce(f32[256]{0:T(256)S(1)} %add_add_fusion, f32[]{:T(128)S(6)} %mul.142), channel_id=1, replica_groups=mesh['groups'=2,'zone'=4,'scen'=2,'hour'=2] {'zone','hour'}, use_global_device_ids=true, to_apply=%region_3.4 | all-reduce | flops 257 | bytes 2056 | tf_op jit(solution)/shard_map/psum | solution.py:69
  108.5 1.2 fusion.94
  109.8 1.3 exponential_reduce_fusion
  111.0 0.6 dynamic-slice
  111.6 1.3 dynamic-update-slice.1
  112.9 1.3 dynamic-update-slice
  114.2 5.1 %all-reduce.4 = (f32[2]{0:T(128)S(1)}, f32[2]{0:T(128)S(1)}) all-reduce(f32[2]{0:T(128)S(1)} %dynamic-update-slice.1, f32[2]{0:T(128)S(1)} %dynamic-update-slice), channel_id=1, replica_groups=mesh['groups'=2,'zone'=4,'scen'=2,'hour'=2] {'scen'}, use_global_device_ids=true, to_apply=%add.1 | all-reduce | flops 4 | bytes 32
  119.3 0.6 fusion.100
  122.5 0.6 fusion.99
  125.1 8.3 %fusion.72 = f32[64,1024]{1,0:T(8,128)S(1)} fusion(bf16[256,8,64]{0,2,1:T(8,128)(2,1)S(1)} %copy.35, f32[8,1024,256]{2,1,0:T(8,128)} %get-tuple-element.44, f32[256]{0:T(256)S(1)} %exponential_divide_fusion, f32[8,1024]{1,0:T(8,128)S(1)} %get-tuple-element.35, f32[8,1024]{1,0:T(8,128)S(1)} %get-tuple-element.52, f32[8,1024]{1,0:T(8,128)S(1)} %get-tuple-element.29, ...), kind=kOutput, calls=%fused_computation.97 | convolution fusion | flops 295108608 | bytes 10060800 | tf_op jit(solution)/shard_map/shp,hsz->hpz/dot_general | solution.py:91
  133.5 6.3 %fusion.74 = f32[64,1024]{1,0:T(8,128)S(1)} fusion(bf16[256,8,64]{0,2,1:T(8,128)(2,1)S(1)} %copy.33, f32[8,1024,256]{2,1,0:T(8,128)S(1)} %copy-done.9, f32[256]{0:T(256)S(1)} %exponential_divide_fusion, f32[8,1024]{1,0:T(8,128)S(1)} %get-tuple-element.36, f32[8,1024]{1,0:T(8,128)S(1)} %get-tuple-element.51, f32[8,1024]{1,0:T(8,128)S(1)} %get-tuple-element.30, ...), kind=kOutput, calls=%fused_computation.101 | convolution fusion | flops 295108608 | bytes 10060800 | tf_op jit(solution)/shard_map/shp,hsz->hpz/dot_general | solution.py:91
  139.9 6.3 %fusion.73 = f32[64,1024]{1,0:T(8,128)S(1)} fusion(bf16[256,8,64]{0,2,1:T(8,128)(2,1)S(1)} %copy.34, f32[8,1024,256]{2,1,0:T(8,128)S(1)} %bitcast.233, f32[256]{0:T(256)S(1)} %exponential_divide_fusion, f32[8,1024]{1,0:T(8,128)S(1)} %get-tuple-element.34, f32[8,1024]{1,0:T(8,128)S(1)} %get-tuple-element.53, f32[8,1024]{1,0:T(8,128)S(1)} %get-tuple-element.28, ...), kind=kOutput, calls=%fused_computation.99 | convolution fusion | flops 295108608 | bytes 10060800 | tf_op jit(solution)/shard_map/shp,hsz->hpz/dot_general | solution.py:91
  146.2 0.6 convolution_multiply_fusion
  146.8 57.6 %all-reduce.2 = f32[64,64]{1,0:T(8,128)S(1)} all-reduce(f32[64,64]{1,0:T(8,128)S(1)} %convolution_multiply_fusion), channel_id=2, replica_groups=mesh['groups'=2,'zone'=4,'scen'=2,'hour'=2] {'zone','scen','hour'}, use_global_device_ids=true, to_apply=%region_12.13.clone | all-reduce | flops 4096 | bytes 32768
  204.4 0.6 dynamic-slice.2
  205.7 0.6 constant_dynamic-slice_fusion
  (40 shorter events, 1.0 us)
Async XLA Ops:
  0.6 45.3 %copy-start = (f32[64,64]{1,0:T(8,128)S(1)}, f32[64,64]{1,0:T(8,128)}, u32[]{:S(2)}) copy-start(f32[64,64]{1,0:T(8,128)} %param.9) | copy-start | bytes 49156
  0.6 40.5 %copy-start.3 = (f32[1024]{0:T(1024)S(1)}, f32[1024]{0:T(1024)}, u32[]{:S(2)}) copy-start(f32[1024]{0:T(1024)} %param.13) | copy-start | bytes 12292
  0.7 40.6 %copy-start.2 = (s32[24,1024]{1,0:T(8,128)S(1)}, s32[24,1024]{1,0:T(8,128)}, u32[]{:S(2)}) copy-start(s32[24,1024]{1,0:T(8,128)} %param.12) | copy-start | bytes 294916
  0.7 40.6 %copy-start.4 = (s32[1024]{0:T(1024)S(1)}, s32[1024]{0:T(1024)}, u32[]{:S(2)}) copy-start(s32[1024]{0:T(1024)} %param.10) | copy-start | bytes 12292
  0.7 40.7 %copy-start.1 = (s32[1024]{0:T(1024)S(1)}, s32[1024]{0:T(1024)}, u32[]{:S(2)}) copy-start(s32[1024]{0:T(1024)} %param.11) | copy-start | bytes 12292
  2.9 4.9 %all-to-all-start = ((bf16[2,2,24576]{2,1,0:T(2,128)(2,1)}), bf16[2,2,24576]{2,1,0:T(2,128)(2,1)S(1)}, u32[]{:S(2)}, u32[]{:S(2)}) async-start(bf16[2,2,24576]{2,1,0:T(2,128)(2,1)} %reshape.77), calls=%async_computation | async-start | bytes 393216 | tf_op jit(solution)/shard_map/all_to_all | solution.py:42
  51.7 13.8 %copy-start.5 = (bf16[24,64,1024]{2,1,0:T(8,128)(2,1)S(1)}, bf16[24,64,1024]{2,1,0:T(8,128)(2,1)}, u32[]{:S(2)}) copy-start(bf16[24,64,1024]{2,1,0:T(8,128)(2,1)} %param.8) | copy-start | bytes 9437188
  78.8 32.3 %copy-start.8 = (u32[32]{0:T(128)S(1)}, u32[32]{0:T(128)}, u32[]{:S(2)}) copy-start(u32[32]{0:T(128)} %constant.81) | copy-start | bytes 388
  125.1 8.4 %copy-start.6 = (bf16[24,64,1024]{2,1,0:T(8,128)(2,1)S(1)}, bf16[24,64,1024]{2,1,0:T(8,128)(2,1)}, u32[]{:S(2)}) copy-start(bf16[24,64,1024]{2,1,0:T(8,128)(2,1)} %param.8) | copy-start | bytes 9437188
  125.1 8.3 %copy-start.9 = (f32[8,1024,256]{2,1,0:T(8,128)S(1)}, f32[8,1024,256]{2,1,0:T(8,128)}, u32[]{:S(2)}) copy-start(f32[8,1024,256]{2,1,0:T(8,128)} %get-tuple-element.46) | copy-start | bytes 25165828
  125.1 14.7 %slice-start = ((s8[8388608]{0:T(1024)(128)(4,1)}), s8[4194304]{0:T(1024)(128)(4,1)S(1)}, s32[]{:S(2)}) async-start(s8[8388608]{0:T(1024)(128)(4,1)} %bitcast.232), calls=%async_computation.1 | async-start | bytes 8388608
  133.5 6.4 %slice-start.1 = ((s8[8388608]{0:T(1024)(128)(4,1)}), s8[4194304]{0:T(1024)(128)(4,1)S(1)}, s32[]{:S(2)}) async-start(s8[8388608]{0:T(1024)(128)(4,1)} %bitcast.232), calls=%async_computation.2 | async-start | bytes 8388608
  139.9 64.6 %copy-start.7 = (u32[32]{0:T(128)S(1)}, u32[32]{0:T(128)}, u32[]{:S(2)}) copy-start(u32[32]{0:T(128)} %constant.93) | copy-start | bytes 388
where the time goes:
time: 208 us; the launch traced here: 207 us
  blocking collectives  111 us (53%)
  matrix products  61.8 us (30%)
  local copies, waits for them, and re-layouts  17 us (8%)
  between operations  8.65 us (4%)
  other arithmetic  4.05 us (2%)
  starting transfers between devices  3.43 us (2%)
    unnamed x2, blocking collectives  62.7 us
    dot_general x3, matrix products, inside_climate_state(): jnp.einsum('shp,hpz->hsz', record_elements, coeff[initial_clock_time:init...  40.3 us
    all_gather x1, blocking collectives, on_device(): outlook_records = lax.all_gather(mine, 'zone', axis=0, tiled=True)  31.7 us
    dot_general x3, matrix products, on_device(): jnp.einsum('shp,hsz->hpz', record_elements, adjoint, preferred_element_ty...  20.9 us
    psum x1, blocking collectives, on_device(): loss_sum, weight_total = lax.psum((sums, weight_part), ('zone', 'hour'))  16.5 us
    unnamed x37, local copies, waits for them, and re-layouts  7.84 us
    gather x1, local copies, waits for them, and re-layouts, on_device(): candidate_plan = jnp.take(owner_ids, building_map)  4.53 us
  transfers between devices with their start and end apart: 1, of which 1 were waited for; matrix products, arithmetic and copies ran while one was open for 0% of the time, Pallas kernels for 0%

commit v1 on v0

v1 whole, which is shorter than its diff:
```python
import functools
import math

import jax
import jax.numpy as jnp
from jax import lax
from jax.experimental import pallas as pl
from jax.experimental.pallas import tpu as pltpu
from jax.sharding import PartitionSpec as P

SHARPNESS = 200.0
LOG2E = 1.4426950408889634
LN2 = 0.6931471805599453
CROSS = 2.0 * math.cosh(0.5)
HIGH = lax.Precision.HIGHEST
MESH = pl.DeviceIdType.MESH
TN = (((0,), (0,)), ((), ()))
NT = (((1,), (1,)), ((), ()))


def split3(x):
    hi = x.astype(jnp.bfloat16)
    rest = x - hi.astype(jnp.float32)
    mid = rest.astype(jnp.bfloat16)
    lo = (rest - mid.astype(jnp.float32)).astype(jnp.bfloat16)
    return hi, mid, lo


def kernel(
    zn, sn, hn, gathered, hours_total,
    fx_ref, resp_hbm, wp_ref, map_ref, own_ref, band_ref, floor_ref,
    sens_ref, obj_ref,
    f_all, resp, ft, slope, prm, plan, wcol, acc, zg, sums, parts, rbuf,
    resp_sem, own_sem, fsend, frecv, ssend, srecv, rsend, rrecv,
):
    n = zn * sn * hn
    my_z = lax.axis_index("zone")
    my_s = lax.axis_index("scen")
    my_h = lax.axis_index("hour")
    me = (my_z * sn + my_s) * hn + my_h
    hours, width, zones = resp.shape
    chunks, slots, per, rows, lanes = f_all.shape
    scens = slots * rows

    resp_copy = pltpu.make_async_copy(resp_hbm, resp, resp_sem)
    resp_copy.start()

    def at(i):
        return {"zone": i // (sn * hn), "scen": (i // hn) % sn, "hour": i % hn}

    barrier = pltpu.get_barrier_semaphore()

    def greet(k, c):
        pl.semaphore_signal(barrier, inc=1, device_id=at((me + k) % n), device_id_type=MESH)
        return c

    lax.fori_loop(1, n, greet, 0)
    pl.semaphore_wait(barrier, n - 1)

    mine = my_z * hn + my_h

    def feed(c, k):
        peer = (mine + k) % slots
        pz, ph = peer // hn, peer % hn
        return pltpu.make_async_remote_copy(
            src_ref=fx_ref.at[ph * chunks + c],
            dst_ref=f_all.at[c, mine],
            send_sem=fsend.at[c, k],
            recv_sem=frecv.at[c, k],
            device_id={"zone": pz, "hour": ph},
            device_id_type=MESH,
        )

    if gathered:
        own_copies = []
        for c in range(chunks):
            own_copies.append(pltpu.make_async_copy(fx_ref.at[c], f_all.at[c, 0], own_sem.at[c]))
            own_copies[-1].start()
    else:
        own_copies = []
        for c in range(chunks):
            cp = pltpu.make_async_copy(fx_ref.at[my_h * chunks + c], f_all.at[c, mine], own_sem.at[c])
            cp.start()
            own_copies.append(cp)
            for k in range(1, slots):
                feed(c, k).start()

    buildings = own_ref.shape[1]
    bstep = min(buildings, 1024)
    zmap = map_ref[...]
    row16 = lax.broadcasted_iota(jnp.int32, (16, bstep), 0)

    def find(i, total):
        start = pl.multiple_of(i * bstep, bstep)
        own = own_ref[:, pl.ds(start, bstep)]
        high = own // 128
        digits = jnp.where(row16 == 0, high, jnp.where(row16 == 1, own - high * 128, 0))
        digits = digits.astype(jnp.float32).astype(jnp.bfloat16)
        ids = lax.broadcasted_iota(jnp.int32, (bstep, zones), 0) + start
        hot = (ids == zmap).astype(jnp.float32).astype(jnp.bfloat16)
        return total + jnp.dot(digits, hot, preferred_element_type=jnp.float32)

    found = lax.fori_loop(0, buildings // bstep, find, jnp.zeros((16, zones), jnp.float32))
    owner = found[0:1, :] * 128.0 + found[1:2, :]
    plan[...] = owner.astype(jnp.int32)

    designs = wp_ref.shape[0]
    dstep = min(designs, 64)

    def pick(i, total):
        start = pl.multiple_of(i * dstep, dstep)
        ids = lax.broadcasted_iota(jnp.int32, (dstep, zones), 0) + start
        hot = (ids == plan[...]).astype(jnp.float32).astype(jnp.bfloat16)
        for piece in split3(wp_ref[pl.ds(start, dstep), :]):
            total = total + lax.dot_general(piece, hot, TN, preferred_element_type=jnp.float32)
        return total

    prm[...] = lax.fori_loop(0, designs // dstep, pick, jnp.zeros((width, zones), jnp.float32))

    acc[...] = jnp.zeros_like(acc)
    lane = lax.broadcasted_iota(jnp.int32, (scens, lanes), 1)
    pad_row = lax.broadcasted_iota(jnp.int32, (width, zones), 0)
    hour_first = my_h * hours

    def occupancy(h):
        position = (hour_first + h).astype(jnp.float32)
        return 1.0 + 2.0 * position / (hours_total - 1)

    resp_copy.wait()
    row_tile, zone_tile = min(64, scens), 256

    for c in range(chunks):
        own_copies[c].wait()
        if not gathered:
            for k in range(1, slots):
                feed(c, k).wait()

        def pair_body(k, carry):
            j = c * per + k
            f2 = f_all[c, :, pl.ds(k, 1), :, :].reshape(scens, lanes)
            ft[j] = f2.astype(jnp.float32).T
            for half in range(2):
                h = 2 * j + half
                coeff = (resp[h].astype(jnp.float32) * prm[...]).astype(jnp.bfloat16)
                mid = 0.25 * (band_ref[pl.ds(h, 1), :].astype(jnp.float32) - 3.5)
                pad = jnp.where(pad_row == 0, -mid, 0.0).astype(jnp.bfloat16)
                if half == 0:
                    left = jnp.where(lane < width, f2.astype(jnp.float32), jnp.where(lane == width, 1.0, 0.0))
                    wcol[half] = jnp.concatenate([coeff, pad], axis=0)
                else:
                    left = jnp.where(lane >= width, f2.astype(jnp.float32), jnp.where(lane == 0, 1.0, 0.0))
                    wcol[half] = jnp.concatenate([pad, coeff], axis=0)
                left = left.astype(jnp.bfloat16)
                weight = floor_ref[...] * occupancy(h)
                for zt in range(zones // zone_tile):
                    zs = slice(zt * zone_tile, (zt + 1) * zone_tile)
                    w_tile = weight[:, zs]
                    for st in range(scens // row_tile):
                        ss = slice(st * row_tile, (st + 1) * row_tile)
                        u = jnp.dot(left[ss, :], wcol[half, :, zs], preferred_element_type=jnp.float32)
                        a = jnp.abs(u) * (-LOG2E)
                        t = jnp.exp2(a)
                        q = t * (t + CROSS) + 1.0
                        cost = (jnp.log2(q) - a) * w_tile
                        part = cost[:, 0:128]
                        for i in range(1, zone_tile // 128):
                            part = part + cost[:, i * 128:(i + 1) * 128]
                        acc[ss, :] += part
                        ub = (u * 0.5).astype(jnp.bfloat16)
                        slope[h, ss, zs] = jnp.tanh(ub - 0.25) + jnp.tanh(ub + 0.25)
            return carry

        lax.fori_loop(0, per, pair_body, 0)

    ones = jnp.ones((8, 128), jnp.float32)
    mysum = lax.dot_general(ones, acc[...], NT, precision=HIGH, preferred_element_type=jnp.float32)[0:1, :]
    floor_sum = jnp.sum(floor_ref[...], axis=1, keepdims=True)
    occ_sum = hours + 2.0 / (hours_total - 1) * (
        hours * hour_first.astype(jnp.float32) + hours * (hours - 1) / 2.0
    )
    mw = floor_sum * occ_sum
    mysum = (mysum * LN2) - 0.5 * mw
    slot = my_z * hn + my_h
    sums[my_s, slot] = jnp.concatenate([mysum, jnp.broadcast_to(mw, (1, 128))], axis=1)

    def tell(k):
        return pltpu.make_async_remote_copy(
            src_ref=sums.at[my_s, slot],
            dst_ref=sums.at[my_s, slot],
            send_sem=ssend.at[k],
            recv_sem=srecv.at[k],
            device_id=at((me + k) % n),
            device_id_type=MESH,
        )

    def tell_start(k, c):
        tell(k).start()
        return c

    def heard(k):
        peer = (me + n - k) % n
        ref = sums.at[(peer // hn) % sn, (peer // (sn * hn)) * hn + peer % hn]
        return pltpu.make_async_remote_copy(
            src_ref=ref, dst_ref=ref, send_sem=ssend.at[k], recv_sem=srecv.at[k],
            device_id=at((me + k) % n), device_id_type=MESH,
        )

    def tell_wait(k, c):
        heard(k).wait_recv()
        return c

    def tell_sent(k, c):
        tell(k).wait_send()
        return c

    lax.fori_loop(1, n, tell_start, 0)
    lax.fori_loop(1, n, tell_wait, 0)

    totals = [jnp.sum(sums[s], axis=0) for s in range(sn)]
    wt = totals[0][:, scens:scens + 1]
    scores = [SHARPNESS * t[:, :scens] / wt for t in totals]
    peak = jnp.max(scores[0], axis=1, keepdims=True)
    for s in scores[1:]:
        peak = jnp.maximum(peak, jnp.max(s, axis=1, keepdims=True))
    exp_total = jnp.sum(jnp.exp(scores[0] - peak), axis=1, keepdims=True)
    for s in scores[1:]:
        exp_total = exp_total + jnp.sum(jnp.exp(s - peak), axis=1, keepdims=True)
    obj_ref[...] = jnp.broadcast_to((peak + jnp.log(exp_total)) / SHARPNESS, obj_ref.shape)
    my_total = jnp.sum(sums[my_s], axis=0)
    sw = jnp.exp(SHARPNESS * my_total[:, :scens] / wt - peak) / exp_total
    lax.fori_loop(1, n, tell_sent, 0)

    zg[...] = jnp.zeros_like(zg)

    def mix_body(j, carry):
        for half in range(2):
            h = 2 * j + half
            fw = ft[j, half * width:(half + 1) * width, :] * (sw * occupancy(h))
            hi = fw.astype(jnp.bfloat16)
            lo = (fw - hi.astype(jnp.float32)).astype(jnp.bfloat16)
            both = jnp.concatenate([hi, lo], axis=0)
            mixed = jnp.dot(both, slope[h], preferred_element_type=jnp.float32)
            zg[...] += resp[h].astype(jnp.float32) * (mixed[:width] + mixed[width:])
        return carry

    lax.fori_loop(0, hours // 2, mix_body, 0)

    zones_all = zones * zn
    gain = 0.5 * math.sqrt(width * zones_all * hours_total * designs)
    pieces = split3(zg[...] * floor_ref[...] * (gain / wt))
    each = designs // n
    block = 8 * min(n, 16)

    def own_body(i, carry):
        r = lax.broadcasted_iota(jnp.int32, (block, zones), 0) + i * block
        ids = jnp.where(r % 8 < each, (r // 8) * each + r % 8, -1)
        hot = (ids == plan[...]).astype(jnp.float32).astype(jnp.bfloat16)
        total = jnp.zeros((block, width), jnp.float32)
        for piece in pieces:
            total = total + lax.dot_general(hot, piece, NT, preferred_element_type=jnp.float32)
        for b in range(block // 8):
            parts[i * (block // 8) + b] = total[b * 8:(b + 1) * 8, :]
        return carry

    lax.fori_loop(0, n // (block // 8), own_body, 0)

    def give(k):
        peer = (me + k) % n
        return pltpu.make_async_remote_copy(
            src_ref=parts.at[peer],
            dst_ref=rbuf.at[k],
            send_sem=rsend.at[k],
            recv_sem=rrecv.at[k],
            device_id=at(peer),
            device_id_type=MESH,
        )

    def give_start(k, c):
        give(k).start()
        return c

    def give_wait(k, c):
        give(k).wait()
        return c

    lax.fori_loop(1, n, give_start, 0)
    rbuf[0] = parts[me]
    lax.fori_loop(1, n, give_wait, 0)
    sens_ref[...] = jnp.sum(rbuf[...], axis=0)[:each, :]


def on_device(forcing, response, window_params, building_map, owner_ids, band_ids, floor_area):
    zn, sn, hn = lax.axis_size("zone"), lax.axis_size("scen"), lax.axis_size("hour")
    n = zn * sn * hn
    hours, width, zones = response.shape
    rows = forcing.shape[0]
    pairs = hours // 2
    gathered = rows % 16 != 0
    if gathered:
        chunks, slots, rows_in = 1, 1, rows * zn * hn
        mine = lax.all_to_all(forcing, "hour", split_axis=1, concat_axis=0, tiled=True)
        whole = lax.all_gather(mine, "zone", axis=0, tiled=True)
        fx = whole.reshape(rows_in, pairs, 2 * width).transpose(1, 0, 2)[None]
    else:
        chunks, slots, rows_in = 4, zn * hn, rows
        fx = forcing.reshape(rows, hn * pairs, 2 * width).transpose(1, 0, 2)
        fx = fx.reshape(hn * chunks, pairs // chunks, rows, 2 * width)
    per = pairs // chunks
    scens = slots * rows_in
    designs = window_params.shape[0]
    vm = pl.BlockSpec(memory_space=pltpu.VMEM)
    anyspace = pl.BlockSpec(memory_space=pl.ANY)
    dma = pltpu.SemaphoreType.DMA
    f32, bf16 = jnp.float32, jnp.bfloat16
    sens, obj = pl.pallas_call(
        functools.partial(kernel, zn, sn, hn, gathered, hours * hn),
        out_shape=(
            jax.ShapeDtypeStruct((designs // n, width), f32),
            jax.ShapeDtypeStruct((1, 128), f32),
        ),
        in_specs=[anyspace, anyspace, vm, vm, vm, vm, vm],
        out_specs=(vm, vm),
        scratch_shapes=[
            pltpu.VMEM((chunks, slots, per, rows_in, 2 * width), bf16),
            pltpu.VMEM((hours, width, zones), bf16),
            pltpu.VMEM((pairs, 2 * width, scens), f32),
            pltpu.VMEM((hours, scens, zones), bf16),
            pltpu.VMEM((width, zones), f32),
            pltpu.VMEM((1, zones), jnp.int32),
            pltpu.VMEM((2, 2 * width, zones), bf16),
            pltpu.VMEM((scens, 128), f32),
            pltpu.VMEM((width, zones), f32),
            pltpu.VMEM((sn, zn * hn, 1, scens + 128), f32),
            pltpu.VMEM((n, 8, width), f32),
            pltpu.VMEM((n, 8, width), f32),
            dma,
            dma((chunks,)),
            dma((chunks, slots)),
            dma((chunks, slots)),
            dma((n,)),
            dma((n,)),
            dma((n,)),
            dma((n,)),
        ],
        compiler_params=pltpu.CompilerParams(
            collective_id=0, has_side_effects=True, vmem_limit_bytes=56 * 1024 * 1024
        ),
        cost_estimate=pl.CostEstimate(
            flops=6 * scens * hours * width * zones,
            bytes_accessed=2 * hours * width * zones,
            transcendentals=4 * scens * hours * zones,
        ),
    )(
        fx, response, window_params, building_map.reshape(1, -1), owner_ids.reshape(1, -1),
        band_ids, floor_area.reshape(1, -1),
    )
    return (sens, obj[0, :1])


def solution(mesh):
    in_specs = (
        P(("groups", "zone", "scen", "hour"), None, None),
        P("hour", None, ("groups", "zone")),
        P("groups", None),
        P(("groups", "zone")),
        P("groups"),
        P("hour", ("groups", "zone")),
        P(("groups", "zone")),
    )
    out_specs = (P(("groups", "zone", "scen", "hour"), None), P("groups"))
    return jax.shard_map(
        on_device, mesh=mesh, in_specs=in_specs, out_specs=out_specs, check_vma=False
    )
```

time: 208 us -> 54.1 us (0.26)
  blocking collectives: 111 us -> 0 us
  matrix products: 61.8 us -> 0 us
  Pallas kernels: 0 us -> 48.4 us
  local copies, waits for them, and re-layouts: 17 us -> 3.17 us
  between operations: 8.65 us -> 2.33 us
  other arithmetic: 4.05 us -> 0 us
  starting transfers between devices: 3.43 us -> 0 us
    unnamed x2 -> x0, blocking collectives: 62.7 us -> none
    dot_general x7 -> x0, matrix products: 61.8 us -> none  [the longest x3 40.3 us: inside_climate_state(): jnp.einsum('shp,hpz->hsz', record_elements, coeff[initial_clock_time:init...]
    pallas_call x0 -> x1, Pallas kernels: none -> 48.4 us  [on_device(): pl.pallas_call(functools.partial(kernel, zn, sn, hn, gathered, hours * hn...]
    all_gather x1 -> x0, blocking collectives: 31.7 us -> none  [on_device(): outlook_records = lax.all_gather(mine, 'zone', axis=0, tiled=True)]
    psum x1 -> x0, blocking collectives: 16.5 us -> none  [on_device(): loss_sum, weight_total = lax.psum((sums, weight_part), ('zone', 'hour'))]
    gather x2 -> x0, local copies, waits for them, and re-layouts: 7.34 us -> none  [the longest x1 4.53 us: on_device(): candidate_plan = jnp.take(owner_ids, building_map)]
    unnamed x37 -> x1, local copies, waits for them, and re-layouts: 7.84 us -> 1.23 us
    all_to_all x1 -> x0, starting transfers between devices: 3.43 us -> none  [on_device(): lax.all_to_all(forcing, 'hour', split_axis=1, concat_axis=0, tiled=True)]
  transfers between devices with their start and end apart: 1 -> 0, of which waited for: 1 -> 0; matrix products, arithmetic and copies ran while one was open for 0% -> 0% of each run, Pallas kernels for 0% -> 0%
where the time goes in v1:
time: 54.1 us; the launch traced here: 53.9 us
  Pallas kernels  48.4 us (89%)
  local copies, waits for them, and re-layouts  3.17 us (6%)
  between operations  2.33 us (4%)
    pallas_call x1, Pallas kernels, on_device(): pl.pallas_call(functools.partial(kernel, zn, sn, hn, gathered, hours * hn...  48.4 us
    reshape x2, local copies, waits for them, and re-layouts, on_device(): fx = forcing.reshape(rows, hn * pairs, 2 * width).transpose(1, 0, 2)  1.94 us
    unnamed x1, local copies, waits for them, and re-layouts  1.23 us

profile of v1, /device:TPU:0, one launch (start us, length us, event | category | flops | bytes accessed | tf_op | source)
XLA Modules:
  0.0 53.9 jit_solution(4851529146553688818)
XLA Ops:
  0.6 1.2 %reshape.19 = bf16[32,24,128]{2,1,0:T(8,128)(2,1)S(1)} reshape(bf16[32,48,64]{2,1,0:T(8,128)(2,1)} %param.7) | data formatting | bytes 393216 | tf_op jit(solution)/shard_map/reshape | solution.py:306
  1.9 0.7 %copy.9 = bf16[32,24,128]{2,0,1:T(8,128)(2,1)} copy(bf16[32,24,128]{2,1,0:T(8,128)(2,1)S(1)} %reshape.19) | data formatting | bytes 393216 | tf_op jit(solution)/shard_map/reshape | solution.py:306
  2.6 48.4 %shard_map.86 = (f32[4,64]{1,0:T(4,128)}, f32[1,128]{1,0:T(1,128)}) custom-call(bf16[8,3,32,128]{3,2,1,0:T(8,128)(2,1)} %bitcast.8, bf16[24,64,1024]{2,1,0:T(8,128)(2,1)} %resp_hbm.1, f32[64,64]{1,0:T(8,128)} %wp_ref.1, s32[1,1024]{1,0:T(1,128)} %bitcast.9, s32[1,1024]{1,0:T(1,128)} %bitcast.10, s32[24,1024]{1,0:T(8,128)} %band_ref.1, f32[1,1024]{1,0:T(1,128)} %bitcast.11), custom_call_target="tpu_custom_call" | custom-call | flops 2415919104 | bytes 3145728 | tf_op jit(solution)/shard_map/pallas_call | solution.py:315
  51.0 1.2 %copy.12 = f32[4,64]{1,0:T(4,128)} copy(f32[4,64]{1,0:T(4,128)} %get-tuple-element.8) | data formatting | bytes 2048

commit v2 on v1

--- a/solution.py
+++ b/solution.py
@@ -14,6 +14,7 @@
 CROSS = 2.0 * math.cosh(0.5)
 HIGH = lax.Precision.HIGHEST
 MESH = pl.DeviceIdType.MESH
+AHEAD = 2
 TN = (((0,), (0,)), ((), ()))
 NT = (((1,), (1,)), ((), ()))
 
@@ -24,6 +25,11 @@
     mid = rest.astype(jnp.bfloat16)
     lo = (rest - mid.astype(jnp.float32)).astype(jnp.bfloat16)
     return hi, mid, lo
+
+
+def chunk_cuts(pairs):
+    sizes = [2] * (pairs // 2) + [1] * (pairs % 2)
+    return [(sum(sizes[:i]), size) for i, size in enumerate(sizes)]
 
 
 def kernel(
@@ -39,51 +45,70 @@
     my_h = lax.axis_index("hour")
     me = (my_z * sn + my_s) * hn + my_h
     hours, width, zones = resp.shape
-    chunks, slots, per, rows, lanes = f_all.shape
+    pairs, slots, rows, lanes = f_all.shape
+    cuts = chunk_cuts(pairs)
     scens = slots * rows
 
     resp_copy = pltpu.make_async_copy(resp_hbm, resp, resp_sem)
     resp_copy.start()
 
-    def at(i):
-        return {"zone": i // (sn * hn), "scen": (i // hn) % sn, "hour": i % hn}
+    def each_peer(body):
+        if n <= 32:
+            for k in range(1, n):
+                body(k)
+        else:
+            lax.fori_loop(1, n, lambda k, c: (body(k), c)[1], 0)
+
+    def away(k, sign=1):
+        dz, ds, dh = k // (sn * hn), (k // hn) % sn, k % hn
+        if sign < 0:
+            dz, ds, dh = zn - dz, sn - ds, hn - dh
+        return (my_z + dz) % zn, (my_s + ds) % sn, (my_h + dh) % hn
+
+    def at(k):
+        z, s, h = away(k)
+        return {"zone": z, "scen": s, "hour": h}
 
     barrier = pltpu.get_barrier_semaphore()
 
-    def greet(k, c):
-        pl.semaphore_signal(barrier, inc=1, device_id=at((me + k) % n), device_id_type=MESH)
-        return c
-
-    lax.fori_loop(1, n, greet, 0)
+    def greet(k):
+        pl.semaphore_signal(barrier, inc=1, device_id=at(k), device_id_type=MESH)
+
+    each_peer(greet)
     pl.semaphore_wait(barrier, n - 1)
 
     mine = my_z * hn + my_h
 
     def feed(c, k):
-        peer = (mine + k) % slots
-        pz, ph = peer // hn, peer % hn
+        first, count = cuts[c]
+        pz, ph = (my_z + k // hn) % zn, (my_h + k % hn) % hn
         return pltpu.make_async_remote_copy(
-            src_ref=fx_ref.at[ph * chunks + c],
-            dst_ref=f_all.at[c, mine],
+            src_ref=fx_ref.at[pl.ds(ph * pairs + first, count)],
+            dst_ref=f_all.at[pl.ds(first, count), mine],
             send_sem=fsend.at[c, k],
             recv_sem=frecv.at[c, k],
             device_id={"zone": pz, "hour": ph},
             device_id_type=MESH,
         )
 
-    if gathered:
-        own_copies = []
-        for c in range(chunks):
-            own_copies.append(pltpu.make_async_copy(fx_ref.at[c], f_all.at[c, 0], own_sem.at[c]))
-            own_copies[-1].start()
-    else:
-        own_copies = []
-        for c in range(chunks):
-            cp = pltpu.make_async_copy(fx_ref.at[my_h * chunks + c], f_all.at[c, mine], own_sem.at[c])
-            cp.start()
-            own_copies.append(cp)
+    own_copies = []
+    for c, (first, count) in enumerate(cuts):
+        start = first if gathered else my_h * pairs + first
+        cp = pltpu.make_async_copy(
+            fx_ref.at[pl.ds(start, count)],
+            f_all.at[pl.ds(first, count), 0 if gathered else mine],
+            own_sem.at[c],
+        )
+        cp.start()
+        own_copies.append(cp)
+
+    def feed_start(c):
+        if not gathered and c < len(cuts):
             for k in range(1, slots):
                 feed(c, k).start()
+
+    for c in range(AHEAD):
+        feed_start(c)
 
     buildings = own_ref.shape[1]
     bstep = min(buildings, 1024)
@@ -127,17 +152,17 @@
         return 1.0 + 2.0 * position / (hours_total - 1)
 
     resp_copy.wait()
-    row_tile, zone_tile = min(64, scens), 256
-
-    for c in range(chunks):
+    row_tile, zone_tile = min(256, scens), 256
+
+    for c, (first, count) in enumerate(cuts):
         own_copies[c].wait()
         if not gathered:
             for k in range(1, slots):
-                feed(c, k).wait()
-
-        def pair_body(k, carry):
-            j = c * per + k
-            f2 = f_all[c, :, pl.ds(k, 1), :, :].reshape(scens, lanes)
+                feed(c, k).wait_recv()
+        feed_start(c + AHEAD)
+
+        def pair_body(j, carry):
+            f2 = f_all[j].reshape(scens, lanes)
             ft[j] = f2.astype(jnp.float32).T
             for half in range(2):
                 h = 2 * j + half
@@ -170,7 +195,12 @@
                         slope[h, ss, zs] = jnp.tanh(ub - 0.25) + jnp.tanh(ub + 0.25)
             return carry
 
-        lax.fori_loop(0, per, pair_body, 0)
+        lax.fori_loop(first, first + count, pair_body, 0)
+
+    if not gathered:
+        for c in range(len(cuts)):
+            for k in range(1, slots):
+                feed(c, k).wait_send()
 
     ones = jnp.ones((8, 128), jnp.float32)
     mysum = lax.dot_general(ones, acc[...], NT, precision=HIGH, preferred_element_type=jnp.float32)[0:1, :]
@@ -189,32 +219,20 @@
             dst_ref=sums.at[my_s, slot],
             send_sem=ssend.at[k],
             recv_sem=srecv.at[k],
-            device_id=at((me + k) % n),
+            device_id=at(k),
             device_id_type=MESH,
         )
 
-    def tell_start(k, c):
-        tell(k).start()
-        return c
-
     def heard(k):
-        peer = (me + n - k) % n
-        ref = sums.at[(peer // hn) % sn, (peer // (sn * hn)) * hn + peer % hn]
+        z, s, h = away(k, -1)
+        ref = sums.at[s, z * hn + h]
         return pltpu.make_async_remote_copy(
             src_ref=ref, dst_ref=ref, send_sem=ssend.at[k], recv_sem=srecv.at[k],
-            device_id=at((me + k) % n), device_id_type=MESH,
-        )
-
-    def tell_wait(k, c):
-        heard(k).wait_recv()
-        return c
-
-    def tell_sent(k, c):
-        tell(k).wait_send()
-        return c
-
-    lax.fori_loop(1, n, tell_start, 0)
-    lax.fori_loop(1, n, tell_wait, 0)
+            device_id=at(k), device_id_type=MESH,
+        )
+
+    each_peer(lambda k: tell(k).start())
+    each_peer(lambda k: heard(k).wait_recv())
 
     totals = [jnp.sum(sums[s], axis=0) for s in range(sn)]
     wt = totals[0][:, scens:scens + 1]
@@ -228,7 +246,7 @@
     obj_ref[...] = jnp.broadcast_to((peak + jnp.log(exp_total)) / SHARPNESS, obj_ref.shape)
     my_total = jnp.sum(sums[my_s], axis=0)
     sw = jnp.exp(SHARPNESS * my_total[:, :scens] / wt - peak) / exp_total
-    lax.fori_loop(1, n, tell_sent, 0)
+    each_peer(lambda k: tell(k).wait_send())
 
     zg[...] = jnp.zeros_like(zg)
 
@@ -265,27 +283,19 @@
     lax.fori_loop(0, n // (block // 8), own_body, 0)
 
     def give(k):
-        peer = (me + k) % n
+        z, s, h = away(k)
         return pltpu.make_async_remote_copy(
-            src_ref=parts.at[peer],
+            src_ref=parts.at[(z * sn + s) * hn + h],
             dst_ref=rbuf.at[k],
             send_sem=rsend.at[k],
             recv_sem=rrecv.at[k],
-            device_id=at(peer),
+            device_id=at(k),
             device_id_type=MESH,
         )
 
-    def give_start(k, c):
-        give(k).start()
-        return c
-
-    def give_wait(k, c):
-        give(k).wait()
-        return c
-
-    lax.fori_loop(1, n, give_start, 0)
+    each_peer(lambda k: give(k).start())
     rbuf[0] = parts[me]
-    lax.fori_loop(1, n, give_wait, 0)
+    each_peer(lambda k: give(k).wait())
     sens_ref[...] = jnp.sum(rbuf[...], axis=0)[:each, :]
 
 
@@ -297,15 +307,14 @@
     pairs = hours // 2
     gathered = rows % 16 != 0
     if gathered:
-        chunks, slots, rows_in = 1, 1, rows * zn * hn
+        slots, rows_in = 1, rows * zn * hn
         mine = lax.all_to_all(forcing, "hour", split_axis=1, concat_axis=0, tiled=True)
         whole = lax.all_gather(mine, "zone", axis=0, tiled=True)
-        fx = whole.reshape(rows_in, pairs, 2 * width).transpose(1, 0, 2)[None]
+        fx = whole.reshape(rows_in, pairs, 2 * width).transpose(1, 0, 2)
     else:
-        chunks, slots, rows_in = 4, zn * hn, rows
+        slots, rows_in = zn * hn, rows
         fx = forcing.reshape(rows, hn * pairs, 2 * width).transpose(1, 0, 2)
-        fx = fx.reshape(hn * chunks, pairs // chunks, rows, 2 * width)
-    per = pairs // chunks
+    chunks = len(chunk_cuts(pairs))
     scens = slots * rows_in
     designs = window_params.shape[0]
     vm = pl.BlockSpec(memory_space=pltpu.VMEM)
@@ -321,7 +330,7 @@
         in_specs=[anyspace, anyspace, vm, vm, vm, vm, vm],
         out_specs=(vm, vm),
         scratch_shapes=[
-            pltpu.VMEM((chunks, slots, per, rows_in, 2 * width), bf16),
+            pltpu.VMEM((pairs, slots, rows_in, 2 * width), bf16),
             pltpu.VMEM((hours, width, zones), bf16),
             pltpu.VMEM((pairs, 2 * width, scens), f32),
             pltpu.VMEM((hours, scens, zones), bf16),

time: 54.1 us -> 50.2 us (0.928)
  Pallas kernels: 48.4 us -> 44.4 us
    pallas_call x1, Pallas kernels: 48.4 us -> 44.4 us  [on_device(): pl.pallas_call(functools.partial(kernel, zn, sn, hn, gathered, hours * hn...]
where the time goes in v2:
time: 50.2 us; the launch traced here: 49.9 us
  Pallas kernels  44.4 us (88%)
  local copies, waits for them, and re-layouts  3.17 us (6%)
  between operations  2.33 us (5%)
    pallas_call x1, Pallas kernels, on_device(): pl.pallas_call(functools.partial(kernel, zn, sn, hn, gathered, hours * hn...  44.4 us
    reshape x2, local copies, waits for them, and re-layouts, on_device(): fx = forcing.reshape(rows, hn * pairs, 2 * width).transpose(1, 0, 2)  1.94 us
    unnamed x1, local copies, waits for them, and re-layouts  1.23 us

profile of v2, /device:TPU:0, one launch (start us, length us, event | category | flops | bytes accessed | tf_op | source)
XLA Modules:
  0.0 49.9 jit_solution(7749324045397593776)
XLA Ops:
  0.6 1.2 %reshape.16 = bf16[32,24,128]{2,1,0:T(8,128)(2,1)S(1)} reshape(bf16[32,48,64]{2,1,0:T(8,128)(2,1)} %param.7) | data formatting | bytes 393216 | tf_op jit(solution)/shard_map/reshape | solution.py:316
  1.9 0.7 %copy.11 = bf16[32,24,128]{2,0,1:T(8,128)(2,1)} copy(bf16[32,24,128]{2,1,0:T(8,128)(2,1)S(1)} %reshape.16) | data formatting | bytes 393216 | tf_op jit(solution)/shard_map/reshape | solution.py:316
  2.6 44.4 %shard_map.86 = (f32[4,64]{1,0:T(4,128)}, f32[1,128]{1,0:T(1,128)}) custom-call(bf16[24,32,128]{2,1,0:T(8,128)(2,1)} %bitcast.8, bf16[24,64,1024]{2,1,0:T(8,128)(2,1)} %resp_hbm.1, f32[64,64]{1,0:T(8,128)} %wp_ref.1, s32[1,1024]{1,0:T(1,128)} %bitcast.9, s32[1,1024]{1,0:T(1,128)} %bitcast.10, s32[24,1024]{1,0:T(8,128)} %band_ref.1, f32[1,1024]{1,0:T(1,128)} %bitcast.11), custom_call_target="tpu_custom_call" | custom-call | flops 2415919104 | bytes 3145728 | tf_op jit(solution)/shard_map/pallas_call | solution.py:324
  47.0 1.2 %copy.14 = f32[4,64]{1,0:T(4,128)} copy(f32[4,64]{1,0:T(4,128)} %get-tuple-element.8) | data formatting | bytes 2048
